TPU v7x, 768 devices: a whole 4x8x12 slice. The times are simulated.
768 devices in a mesh: stream: 192 (over z_hi, x, y, core), span: 4 (over z_lo).
Axes of the slice: x: 4, y: 8, z: 12 (z_hi: 3, z_lo: 4; z = z_hi * 4 + z_lo), core: 2. Of those that a mesh axis runs over, the one named last changes fastest.
Arguments:
- source: float32 [3072, 24, 512], P('stream', None, 'span'), may hold values from -24 to 24
- geometry: bfloat16 [6, 3072, 24, 512], P(None, 'stream', None, 'span'), may hold values from -1.68 to 36, as said below
Outputs:
- solution_field: float32 [3072, 24, 512], P('stream', None, 'span')
- residual: float32 [3072, 24, 512], P('stream', None, 'span')
Inputs may be any that keep to these rules, and one draw needn't show every extreme that they name: `geometry`: at every point the three leading factors are positive and each exceeds the sum of the magnitudes of the two coupling factors of its row.
All inputs are finite; a program needn't handle non-finite values.
Results may differ from a plain program's by a relative error of at most 0.024.
Values sent between devices are 32-bit elements; how exact they have to be, the bound alone decides.
A program may use at most 32 MiB of HBM per device.

v0:
```python
import jax
import jax.numpy as jnp
import numpy as np
from jax import lax
from jax.sharding import PartitionSpec as P

NODES = 8
ITERS = 3


def padded_2(cells, sides, width):
    for axis, dim in sides:
        count = lax.axis_size(axis)
        head = lax.slice_in_dim(cells, 0, width, axis=dim)
        tail = lax.slice_in_dim(cells, cells.shape[dim] - width, cells.shape[dim], axis=dim)
        cells = jnp.concatenate(
            [
                lax.ppermute(tail, axis, [(i, (i + 1) % count) for i in range(count)]),
                cells,
                lax.ppermute(head, axis, [((i + 1) % count, i) for i in range(count)]),
            ],
            axis=dim,
        )
    return cells


def gll_tables():
    gll_points = np.array(
        [
            -1.0,
            -0.8717401485096066,
            -0.5917001814331423,
            -0.2092992179024789,
            0.2092992179024789,
            0.5917001814331423,
            0.8717401485096066,
            1.0,
        ]
    )
    quadrature_weight = np.array(
        [
            1.0 / 28.0,
            0.2107042271435061,
            0.3411226924835044,
            0.4124587946587038,
            0.4124587946587038,
            0.3411226924835044,
            0.2107042271435061,
            1.0 / 28.0,
        ]
    )
    barycentric = np.array(
        [
            1.0 / np.prod([gll_points[j] - gll_points[k] for k in range(8) if k != j])
            for j in range(8)
        ]
    )
    derivative = np.zeros((8, 8))
    for j in range(8):
        for k in range(8):
            if j != k:
                derivative[j, k] = barycentric[k] / barycentric[j] / (gll_points[j] - gll_points[k])
    for j in range(8):
        derivative[j, j] = -np.sum(derivative[j])
    return (quadrature_weight, derivative)


def boundary_half_parts(elements):
    pattern = np.ones(NODES)
    pattern[0] = 0.5
    pattern[NODES - 1] = 0.5
    return np.tile(pattern, elements)


def wall_table(count):
    table = np.ones(count)
    table[0] = 0.0
    table[count - 1] = 0.0
    return table


def pair_faces(interior, lower_plane, upper_plane, axis_dim):
    extent = interior.shape
    elements = extent[axis_dim] // NODES
    blocks = interior.reshape(extent[:axis_dim] + (elements, NODES) + extent[axis_dim + 1 :])
    first_planes = lax.index_in_dim(blocks, 0, axis_dim + 1, keepdims=False)
    last_planes = lax.index_in_dim(blocks, NODES - 1, axis_dim + 1, keepdims=False)
    next_planes = jnp.concatenate(
        [lax.slice_in_dim(first_planes, 1, elements, axis=axis_dim), upper_plane], axis=axis_dim
    )
    face_sums = last_planes + next_planes
    prev_planes = jnp.concatenate(
        [
            lower_plane + lax.slice_in_dim(first_planes, 0, 1, axis=axis_dim),
            lax.slice_in_dim(face_sums, 0, elements - 1, axis=axis_dim),
        ],
        axis=axis_dim,
    )
    middle = lax.slice_in_dim(blocks, 1, NODES - 1, axis=axis_dim + 1)
    joined = jnp.concatenate(
        [
            jnp.expand_dims(prev_planes, axis_dim + 1),
            middle,
            jnp.expand_dims(face_sums, axis_dim + 1),
        ],
        axis=axis_dim + 1,
    )
    return joined.reshape(extent)


def derivative_lead(values, matrix, axis_dim):
    extent = values.shape
    elements = extent[axis_dim] // NODES
    blocks = values.reshape(extent[:axis_dim] + (elements, NODES) + extent[axis_dim + 1 :])
    if axis_dim == 0:
        derived = jnp.einsum("ij,ejyz->eiyz", matrix, blocks, precision=lax.Precision.HIGHEST)
    else:
        derived = jnp.einsum("ij,xejz->xeiz", matrix, blocks, precision=lax.Precision.HIGHEST)
    return derived.reshape(extent)


def assemble(values):
    padded = padded_2(values, (("stream", 0),), 1)
    summed = pair_faces(padded[1:-1], padded[0:1], padded[-1:], 0)
    summed = pair_faces(summed, jnp.zeros_like(summed[:, 0:1]), jnp.zeros_like(summed[:, 0:1]), 1)
    padded = padded_2(summed, (("span", 2),), 1)
    return pair_faces(padded[:, :, 1:-1], padded[:, :, 0:1], padded[:, :, -1:], 2)


def shards(source, geometry):
    quadrature_weight, derivative_table = gll_tables()
    extent = source.shape
    matrix = jnp.asarray(derivative_table, dtype=jnp.float32)
    span_matrix = jnp.asarray(
        np.kron(np.eye(extent[2] // NODES), derivative_table), dtype=jnp.float32
    )
    weight = (
        jnp.asarray(np.tile(quadrature_weight, extent[0] // NODES), dtype=jnp.float32)[
            :, None, None
        ]
        * jnp.asarray(np.tile(quadrature_weight, extent[1] // NODES), dtype=jnp.float32)[
            None, :, None
        ]
        * jnp.asarray(np.tile(quadrature_weight, extent[2] // NODES), dtype=jnp.float32)[
            None, None, :
        ]
    )
    half_parts = (
        jnp.asarray(boundary_half_parts(extent[0] // NODES), dtype=jnp.float32)[:, None, None]
        * jnp.asarray(boundary_half_parts(extent[1] // NODES), dtype=jnp.float32)[None, :, None]
        * jnp.asarray(boundary_half_parts(extent[2] // NODES), dtype=jnp.float32)[None, None, :]
    )
    wall_mask = jnp.asarray(wall_table(extent[1]), dtype=jnp.float32)[None, :, None]
    metric = geometry.astype(jnp.float32)
    couplings = ((0, 3, 4), (3, 1, 5), (4, 5, 2))

    def apply_operator(values):
        gradients = [
            derivative_lead(values, matrix, 0),
            derivative_lead(values, matrix, 1),
            jnp.dot(values, span_matrix.T, precision=lax.Precision.HIGHEST),
        ]
        fluxes = []
        for axis_dim in range(3):
            components = couplings[axis_dim]
            fluxes.append(
                weight
                * (
                    metric[components[0]] * gradients[0]
                    + metric[components[1]] * gradients[1]
                    + metric[components[2]] * gradients[2]
                )
            )
        stiffness = (
            derivative_lead(fluxes[0], matrix.T, 0)
            + derivative_lead(fluxes[1], matrix.T, 1)
            + jnp.dot(fluxes[2], span_matrix, precision=lax.Precision.HIGHEST)
        )
        return wall_mask * assemble(stiffness)

    def two_products(current, applied):
        return lax.psum(
            (jnp.sum(current * current * half_parts), jnp.sum(current * applied * half_parts)),
            ("stream", "span"),
        )

    right_side = wall_mask * assemble(source)
    solution_field = jnp.zeros_like(right_side)
    residual = right_side
    applied = apply_operator(residual)
    norm_now, curvature = two_products(residual, applied)
    step_size = norm_now / curvature
    direction = residual
    applied_dir = applied
    for iteration in range(ITERS):
        solution_field = solution_field + step_size * direction
        residual = residual - step_size * applied_dir
        if iteration + 1 < ITERS:
            applied = apply_operator(residual)
            norm_next, curvature = two_products(residual, applied)
            beta_ratio = norm_next / norm_now
            step_size = norm_next / (curvature - beta_ratio * norm_next / step_size)
            direction = residual + beta_ratio * direction
            applied_dir = applied + beta_ratio * applied_dir
            norm_now = norm_next
    return (solution_field, residual)


def solution(mesh):
    return jax.shard_map(
        shards,
        mesh=mesh,
        in_specs=(P("stream", None, "span"), P(None, "stream", None, "span")),
        out_specs=(P("stream", None, "span"), P("stream", None, "span")),
        check_vma=False,
    )
```

profile of v0, /device:TPU:1, one launch (start us, length us, event | category | flops | bytes accessed | tf_op | source)
XLA Modules:
  0.0 555.2 jit_solution(16719572181540956248)
XLA Ops:
  1.4 12.4 %collective-permute-start.1 = (f32[1,24,128]{2,1,0:T(8,128)S(1)}, f32[1,24,128]{2,1,0:T(8,128)S(1)}, u32[]{:S(2)}, u32[]{:S(2)}) collective-permute-start(f32[1,24,128]{2,1,0:T(8,128)S(1)} %get-tuple-element.93), channel_id=1, source_target_pairs={{4,0},{8,4},{12,8},{16,12},{20,16},{24,20},{28,24},{32,28},{36,32}... | collective-permute-start | bytes 36872 | tf_op jit(solution)/shard_map/ppermute | solution.py:20
  13.8 1.9 collective-permute-start
  19.4 2.2 convert_element_type.3
  22.4 2.2 collective-permute-done
  28.0 3.1 collective-permute-start.2
  33.0 4.0 collective-permute-start.3
  37.9 1.9 collective-permute-done.3
  41.4 1.8 fusion.116
  43.9 2.5 copy.644
  46.4 2.2 copy.638
  48.6 2.2 copy.639
  55.3 1.9 fusion.33
  58.5 13.8 %collective-permute-start.5 = (f32[1,24,128]{2,1,0:T(8,128)S(1)}, f32[1,24,128]{2,1,0:T(8,128)S(1)}, u32[]{:S(2)}, u32[]{:S(2)}) collective-permute-start(f32[1,24,128]{2,1,0:T(8,128)S(1)} %get-tuple-element.81), channel_id=1, source_target_pairs={{4,0},{8,4},{12,8},{16,12},{20,16},{24,20},{28,24},{32,28},{36,32}... | collective-permute-start | bytes 36872 | tf_op jit(solution)/shard_map/ppermute | solution.py:20
  72.3 1.9 collective-permute-start.4
  74.3 4.6 collective-permute-done.4
  84.0 2.8 collective-permute-start.6
  86.8 4.8 collective-permute-start.7
  92.8 2.7 fusion.1
  95.5 2.2 copy.661
  99.9 115.6 %all-reduce.6 = (f32[]{:T(128)}, f32[]{:T(128)}) all-reduce(f32[]{:T(128)} %get-tuple-element.19, f32[]{:T(128)} %get-tuple-element.18), channel_id=1, replica_groups=mesh['stream'=192,'span'=4] {'stream','span'}, use_global_device_ids=true, to_apply=%region_1.0 | all-reduce | flops 2 | bytes 16 | tf_op jit(solution)/shard_map/psum | solution.py:182
  216.8 1.8 multiply_subtract_fusion.5
  218.6 2.1 convolution_bitcast_fusion.6
  220.7 2.2 copy.662
  225.1 1.9 fusion.27
  228.2 2.6 collective-permute-start.9
  230.8 3.0 collective-permute-start.8
  233.9 3.7 collective-permute-done.8
  239.6 1.5 copy.676
  241.2 2.4 copy.750
  246.9 1.9 collective-permute-start.10
  248.9 5.2 collective-permute-start.11
  255.4 3.8 fusion.3
  259.2 118.1 %all-reduce.5 = (f32[]{:T(128)}, f32[]{:T(128)}) all-reduce(f32[]{:T(128)} %get-tuple-element.17, f32[]{:T(128)} %get-tuple-element.16), channel_id=1, replica_groups=mesh['stream'=192,'span'=4] {'stream','span'}, use_global_device_ids=true, to_apply=%region_5.0 | all-reduce | flops 2 | bytes 16 | tf_op jit(solution)/shard_map/psum | solution.py:182
  381.9 3.4 copy.684
  385.3 2.5 copy.688
  387.8 2.2 copy.685
  390.0 2.2 convolution_bitcast_fusion.2
  394.5 2.5 copy.690
  398.2 2.0 fusion.21
  401.5 2.6 collective-permute-start.13
  404.1 3.0 collective-permute-start.12
  407.1 1.7 collective-permute-done.12
  412.3 2.3 copy.754
  418.2 2.4 collective-permute-start.14
  420.6 4.8 collective-permute-start.15
  426.8 4.0 fusion.5
  430.8 117.9 %all-reduce.4 = (f32[]{:T(128)}, f32[]{:T(128)}) all-reduce(f32[]{:T(128)} %get-tuple-element.21, f32[]{:T(128)} %get-tuple-element.20), channel_id=1, replica_groups=mesh['stream'=192,'span'=4] {'stream','span'}, use_global_device_ids=true, to_apply=%region_9.0 | all-reduce | flops 2 | bytes 16 | tf_op jit(solution)/shard_map/psum | solution.py:182
  552.4 1.8 copy.708
  (206 shorter events, 51.4 us)
Async XLA Ops:
  1.4 20.3 %collective-permute-start.1 = (f32[1,24,128]{2,1,0:T(8,128)S(1)}, f32[1,24,128]{2,1,0:T(8,128)S(1)}, u32[]{:S(2)}, u32[]{:S(2)}) collective-permute-start(f32[1,24,128]{2,1,0:T(8,128)S(1)} %get-tuple-element.93), channel_id=1, source_target_pairs={{4,0},{8,4},{12,8},{16,12},{20,16},{24,20},{28,24},{32,28},{36,32}... | collective-permute-start | bytes 36872 | tf_op jit(solution)/shard_map/ppermute | solution.py:20
  13.8 10.7 %collective-permute-start = (f32[1,24,128]{2,1,0:T(8,128)S(1)}, f32[1,24,128]{2,1,0:T(8,128)S(1)}, u32[]{:S(2)}, u32[]{:S(2)}) collective-permute-start(f32[1,24,128]{2,1,0:T(8,128)S(1)} %get-tuple-element.92), channel_id=1, source_target_pairs={{0,4},{4,8},{8,12},{12,16},{16,20},{20,24},{24,28},{28,32},{32,36}... | collective-permute-start | bytes 36872 | tf_op jit(solution)/shard_map/ppermute | solution.py:18
  28.0 9.0 %collective-permute-start.2 = (f32[16,24,1]{2,1,0:T(8,128)}, f32[16,24,1]{2,1,0:T(8,128)}, u32[]{:S(2)}, u32[]{:S(2)}) collective-permute-start(f32[16,24,1]{2,1,0:T(8,128)} %get-tuple-element.86), channel_id=1, source_target_pairs={{0,1},{1,2},{2,3},{3,0},{4,5},{5,6},{6,7},{7,4},{8,9},{9,10},{10,1... | collective-permute-start | bytes 4616 | tf_op jit(solution)/shard_map/ppermute | solution.py:18
  31.9 0.9 copy-start.9
  32.2 9.0 %copy-start.10 = (f32[16,24,15,1]{2,1,0,3:T(8,128)S(1)}, f32[16,24,15,1]{2,1,0,3:T(8,128)}, u32[]{:S(2)}) copy-start(f32[16,24,15,1]{2,1,0,3:T(8,128)} %get-tuple-element.89) | copy-start | bytes 69124
  33.0 6.9 %collective-permute-start.3 = (f32[16,24,1]{2,1,0:T(8,128)}, f32[16,24,1]{2,1,0:T(8,128)S(1)}, u32[]{:S(2)}, u32[]{:S(2)}) collective-permute-start(f32[16,24,1]{2,1,0:T(8,128)} %get-tuple-element.87), channel_id=1, source_target_pairs={{1,0},{2,1},{3,2},{0,3},{5,4},{6,5},{7,6},{4,7},{9,8},{10,9},{11,1... | collective-permute-start | bytes 4616 | tf_op jit(solution)/shard_map/ppermute | solution.py:20
  46.4 4.4 copy-start.20
  46.4 5.4 copy-start.11
  54.0 3.7 copy-start.21
  54.0 4.1 copy-start.3
  58.5 15.8 %collective-permute-start.5 = (f32[1,24,128]{2,1,0:T(8,128)S(1)}, f32[1,24,128]{2,1,0:T(8,128)S(1)}, u32[]{:S(2)}, u32[]{:S(2)}) collective-permute-start(f32[1,24,128]{2,1,0:T(8,128)S(1)} %get-tuple-element.81), channel_id=1, source_target_pairs={{4,0},{8,4},{12,8},{16,12},{20,16},{24,20},{28,24},{32,28},{36,32}... | collective-permute-start | bytes 36872 | tf_op jit(solution)/shard_map/ppermute | solution.py:20
  72.3 6.5 %collective-permute-start.4 = (f32[1,24,128]{2,1,0:T(8,128)S(1)}, f32[1,24,128]{2,1,0:T(8,128)S(1)}, u32[]{:S(2)}, u32[]{:S(2)}) collective-permute-start(f32[1,24,128]{2,1,0:T(8,128)S(1)} %get-tuple-element.80), channel_id=1, source_target_pairs={{0,4},{4,8},{8,12},{12,16},{16,20},{20,24},{24,28},{28,32},{32,36}... | collective-permute-start | bytes 36872 | tf_op jit(solution)/shard_map/ppermute | solution.py:18
  84.0 8.8 %copy-start.12 = (f32[16,24]{0,1:T(8,128)S(1)}, f32[16,24]{0,1:T(8,128)}, u32[]{:S(2)}) copy-start(f32[16,24]{0,1:T(8,128)} %broadcast_multiply_fusion.1) | copy-start | bytes 4612
  84.0 8.8 %copy-start.17 = (f32[16,8]{1,0:T(8,128)S(1)}, f32[16,8]{1,0:T(8,128)}, u32[]{:S(2)}) copy-start(f32[16,8]{1,0:T(8,128)} %constant.40) | copy-start | bytes 1540
  84.0 8.6 %collective-permute-start.6 = (f32[16,24,1]{0,2,1:T(1,128)S(1)}, f32[16,24,1]{0,2,1:T(1,128)S(1)}, u32[]{:S(2)}, u32[]{:S(2)}) collective-permute-start(f32[16,24,1]{0,2,1:T(1,128)S(1)} %get-tuple-element.48), channel_id=1, source_target_pairs={{0,1},{1,2},{2,3},{3,0},{4,5},{5,6},{6,7},{7,4},{8,9},{9,10},{10,1... | collective-permute-start | bytes 4616 | tf_op jit(solution)/shard_map/ppermute | solution.py:18
  86.8 5.4 collective-permute-start.7
  224.0 0.7 copy-start.6
  224.7 2.7 copy-start.22
  225.0 2.8 copy-start.4
  228.2 5.6 %collective-permute-start.9 = (f32[1,24,128]{2,1,0:T(8,128)S(1)}, f32[1,24,128]{2,1,0:T(8,128)S(1)}, u32[]{:S(2)}, u32[]{:S(2)}) collective-permute-start(f32[1,24,128]{2,1,0:T(8,128)S(1)} %get-tuple-element.71), channel_id=1, source_target_pairs={{4,0},{8,4},{12,8},{16,12},{20,16},{24,20},{28,24},{32,28},{36,32}... | collective-permute-start | bytes 36872 | tf_op jit(solution)/shard_map/ppermute | solution.py:20
  230.8 6.7 %collective-permute-start.8 = (f32[1,24,128]{2,1,0:T(8,128)S(1)}, f32[1,24,128]{2,1,0:T(8,128)S(1)}, u32[]{:S(2)}, u32[]{:S(2)}) collective-permute-start(f32[1,24,128]{2,1,0:T(8,128)S(1)} %get-tuple-element.70), channel_id=1, source_target_pairs={{0,4},{4,8},{8,12},{12,16},{16,20},{20,24},{24,28},{28,32},{32,36}... | collective-permute-start | bytes 36872 | tf_op jit(solution)/shard_map/ppermute | solution.py:18
  238.4 0.6 copy-start.15
  246.9 8.5 %copy-start.13 = (f32[16,24]{0,1:T(8,128)S(1)}, f32[16,24]{0,1:T(8,128)}, u32[]{:S(2)}) copy-start(f32[16,24]{0,1:T(8,128)} %broadcast_multiply_fusion.1) | copy-start | bytes 4612
  246.9 8.5 %copy-start.18 = (f32[16,8]{1,0:T(8,128)S(1)}, f32[16,8]{1,0:T(8,128)}, u32[]{:S(2)}) copy-start(f32[16,8]{1,0:T(8,128)} %constant.40) | copy-start | bytes 1540
  246.9 8.3 %collective-permute-start.10 = (f32[16,24,1]{0,2,1:T(1,128)S(1)}, f32[16,24,1]{0,2,1:T(1,128)S(1)}, u32[]{:S(2)}, u32[]{:S(2)}) collective-permute-start(f32[16,24,1]{0,2,1:T(1,128)S(1)} %get-tuple-element.44), channel_id=1, source_target_pairs={{0,1},{1,2},{2,3},{3,0},{4,5},{5,6},{6,7},{7,4},{8,9},{9,10},{10,1... | collective-permute-start | bytes 4616 | tf_op jit(solution)/shard_map/ppermute | solution.py:18
  248.9 6.0 %collective-permute-start.11 = (f32[16,24,1]{0,2,1:T(1,128)S(1)}, f32[16,24,1]{0,2,1:T(1,128)S(1)}, u32[]{:S(2)}, u32[]{:S(2)}) collective-permute-start(f32[16,24,1]{0,2,1:T(1,128)S(1)} %get-tuple-element.45), channel_id=1, source_target_pairs={{1,0},{2,1},{3,2},{0,3},{5,4},{6,5},{7,6},{4,7},{9,8},{10,9},{11,1... | collective-permute-start | bytes 4616 | tf_op jit(solution)/shard_map/ppermute | solution.py:20
  397.0 3.6 copy-start.23
  398.2 3.3 copy-start.7
  398.2 2.9 copy-start.5
  401.5 5.6 %collective-permute-start.13 = (f32[1,24,128]{2,1,0:T(8,128)S(1)}, f32[1,24,128]{2,1,0:T(8,128)S(1)}, u32[]{:S(2)}, u32[]{:S(2)}) collective-permute-start(f32[1,24,128]{2,1,0:T(8,128)S(1)} %get-tuple-element.61), channel_id=1, source_target_pairs={{4,0},{8,4},{12,8},{16,12},{20,16},{24,20},{28,24},{32,28},{36,32}... | collective-permute-start | bytes 36872 | tf_op jit(solution)/shard_map/ppermute | solution.py:20
  404.1 4.7 collective-permute-start.12
  409.6 0.6 copy-start.16
  418.1 8.6 %copy-start = (f32[16,24,16,8]{0,3,2,1:T(8,128)S(1)}, f32[16,24,16,8]{0,3,2,1:T(8,128)}, u32[]{:S(2)}) copy-start(f32[16,24,16,8]{0,3,2,1:T(8,128)} %get-tuple-element.28) | copy-start | bytes 589828
  418.1 8.6 %copy-start.14 = (f32[16,24]{0,1:T(8,128)S(1)}, f32[16,24]{0,1:T(8,128)}, u32[]{:S(2)}) copy-start(f32[16,24]{0,1:T(8,128)} %broadcast_multiply_fusion.1) | copy-start | bytes 4612
  418.1 8.6 %copy-start.19 = (f32[16,8]{1,0:T(8,128)S(1)}, f32[16,8]{1,0:T(8,128)}, u32[]{:S(2)}) copy-start(f32[16,8]{1,0:T(8,128)} %constant.40) | copy-start | bytes 1540
  418.2 8.5 %collective-permute-start.14 = (f32[16,24,1]{0,2,1:T(1,128)S(1)}, f32[16,24,1]{0,2,1:T(1,128)S(1)}, u32[]{:S(2)}, u32[]{:S(2)}) collective-permute-start(f32[16,24,1]{0,2,1:T(1,128)S(1)} %get-tuple-element.40), channel_id=1, source_target_pairs={{0,1},{1,2},{2,3},{3,0},{4,5},{5,6},{6,7},{7,4},{8,9},{9,10},{10,1... | collective-permute-start | bytes 4616 | tf_op jit(solution)/shard_map/ppermute | solution.py:18
  420.6 5.6 %collective-permute-start.15 = (f32[16,24,1]{0,2,1:T(1,128)S(1)}, f32[16,24,1]{0,2,1:T(1,128)S(1)}, u32[]{:S(2)}, u32[]{:S(2)}) collective-permute-start(f32[16,24,1]{0,2,1:T(1,128)S(1)} %get-tuple-element.41), channel_id=1, source_target_pairs={{1,0},{2,1},{3,2},{0,3},{5,4},{6,5},{7,6},{4,7},{9,8},{10,9},{11,1... | collective-permute-start | bytes 4616 | tf_op jit(solution)/shard_map/ppermute | solution.py:20
  430.8 123.4 %copy-start.1 = (f32[16,24,128]{2,1,0:T(8,128)S(1)}, f32[16,24,128]{2,1,0:T(8,128)}, u32[]{:S(2)}) copy-start(f32[16,24,128]{2,1,0:T(8,128)} %copy.644) | copy-start | bytes 589828
  430.8 123.4 %copy-start.2 = (f32[16,24,128]{2,1,0:T(8,128)S(1)}, f32[16,24,128]{2,1,0:T(8,128)}, u32[]{:S(2)}) copy-start(f32[16,24,128]{2,1,0:T(8,128)} %multiply_subtract_fusion.5) | copy-start | bytes 589828
  430.8 123.4 %copy-start.8 = (f32[16,24,128]{2,1,0:T(8,128)S(1)}, f32[16,24,128]{2,1,0:T(8,128)}, u32[]{:S(2)}) copy-start(f32[16,24,128]{2,1,0:T(8,128)} %copy-done.7) | copy-start | bytes 589828
where the time goes:
time: 557 us; the launch traced here: 555 us
  blocking collectives  352 us (63%)
  starting transfers between devices  70.2 us (13%)
  local copies, waits for them, and re-layouts  54.8 us (10%)
  other arithmetic  35.8 us (6%)
  matrix products  15.8 us (3%)
  waiting for transfers between devices  15.7 us (3%)
  between operations  11.4 us (2%)
    psum x3, blocking collectives, two_products(): lax.psum((jnp.sum(current * current * half_parts), jnp.sum(current * appl...  352 us
    ppermute x8, starting transfers between devices, padded_2(): lax.ppermute(head, axis, [((i + 1) % count, i) for i in range(count)])  50.1 us
    ppermute x8, starting transfers between devices, padded_2(): lax.ppermute(tail, axis, [(i, (i + 1) % count) for i in range(count)])  20.1 us
    reshape x10, local copies, waits for them, and re-layouts, pair_faces(): return joined.reshape(extent)  19.4 us
    ppermute x8, waiting for transfers between devices, padded_2(): lax.ppermute(tail, axis, [(i, (i + 1) % count) for i in range(count)])  12.2 us
  transfers between devices with their start and end apart: 16, of which 8 were waited for; matrix products, arithmetic and copies ran while one was open for 2% of the time, Pallas kernels for 0%

commit v1 on v0

v1 whole, which is shorter than its diff:
```python
import functools

import jax
import jax.numpy as jnp
import numpy as np
from jax import lax
from jax.experimental import pallas as pl
from jax.experimental.pallas import tpu as pltpu
from jax.sharding import PartitionSpec as P

MESH = pl.DeviceIdType.MESH
NODES = 8
EX = 2
EY = 3
LANES = 128
ROUNDS = 4
HIGHEST = lax.Precision.HIGHEST
Z_HI, X, Y, CORES, Z_LO = 3, 4, 8, 2, 4
Z = Z_HI * Z_LO


def gll_tables():
    points = np.array(
        [
            -1.0,
            -0.8717401485096066,
            -0.5917001814331423,
            -0.2092992179024789,
            0.2092992179024789,
            0.5917001814331423,
            0.8717401485096066,
            1.0,
        ]
    )
    weights = np.array(
        [
            1.0 / 28.0,
            0.2107042271435061,
            0.3411226924835044,
            0.4124587946587038,
            0.4124587946587038,
            0.3411226924835044,
            0.2107042271435061,
            1.0 / 28.0,
        ]
    )
    barycentric = np.array(
        [
            1.0 / np.prod([points[j] - points[k] for k in range(8) if k != j])
            for j in range(8)
        ]
    )
    derivative = np.zeros((8, 8))
    for j in range(8):
        for k in range(8):
            if j != k:
                derivative[j, k] = barycentric[k] / barycentric[j] / (points[j] - points[k])
    for j in range(8):
        derivative[j, j] = -np.sum(derivative[j])
    return weights, derivative


WEIGHTS, DERIVATIVE = gll_tables()


def constants():
    half = np.ones(NODES)
    half[0] = half[-1] = 0.5
    copies = LANES // NODES
    blocks = np.kron(np.eye(copies), DERIVATIVE)
    weight = WEIGHTS[:, None] * np.tile(WEIGHTS, copies)[None, :]
    halves = half[:, None] * np.tile(half, copies)[None, :]
    return np.concatenate([blocks, blocks.T, weight, halves]).astype(np.float32)


def neighbours(count_s, count_p):
    s, p = lax.axis_index("stream"), lax.axis_index("span")
    down, up = lax.rem(s + count_s - 1, count_s), lax.rem(s + 1, count_s)
    left, right = lax.rem(p + count_p - 1, count_p), lax.rem(p + 1, count_p)
    return s, p, down, up, left, right


def column_peers(s, p):
    core, z_hi = lax.rem(s, CORES), s // (X * Y * CORES)
    base = s - core - z_hi * (X * Y * CORES)
    z = z_hi * Z_LO + p
    peers = []
    for dz in range(Z):
        for dc in range(CORES):
            if dz or dc:
                other = lax.rem(z + dz, Z)
                c = lax.rem(core + dc, CORES)
                peers.append((base + (other // Z_LO) * (X * Y * CORES) + c, lax.rem(other, Z_LO)))
    return peers


def plane_peers(s, p):
    core, row = lax.rem(s, CORES), s // CORES
    y, x, z_hi = lax.rem(row, Y), lax.rem(row // Y, X), row // (X * Y)
    peers = []
    for dx in range(X):
        for dy in range(Y):
            if dx or dy:
                there = (z_hi * X + lax.rem(x + dx, X)) * Y + lax.rem(y + dy, Y)
                peers.append((there * CORES + core, p))
    return peers


def along_x(parts, matrix):
    even = [parts[j] + parts[7 - j] for j in range(4)]
    odd = [parts[j] - parts[7 - j] for j in range(4)]
    low, high = [None] * 4, [None] * 4
    for i in range(4):
        a = sum(odd[j] * float(0.5 * (matrix[i, j] - matrix[i, 7 - j])) for j in range(4))
        b = sum(even[j] * float(0.5 * (matrix[i, j] + matrix[i, 7 - j])) for j in range(4))
        low[i], high[i] = b + a, a - b
    return low + high[::-1]


def kernel(
    count_s,
    count_p,
    source_hbm,
    geometry_hbm,
    constant_hbm,
    solution_ref,
    residual_ref,
    source,
    geometry,
    constant,
    metric,
    fields,
    partial,
    planes,
    packs,
    packed,
    grad1,
    grad2,
    row1,
    row2,
    column,
    plane,
    load_sem,
    send_sem,
    recv_sem,
    sum_send,
    sum_recv,
):
    s, p, down, up, left, right = neighbours(count_s, count_p)
    halo = [(down, p), (up, p), (s, left), (s, right)]
    halo += [(down, left), (down, right), (up, left), (up, right)]
    in_column, in_plane = column_peers(s, p), plane_peers(s, p)

    loads = [
        pltpu.make_async_copy(source_hbm, source, load_sem.at[0]),
        pltpu.make_async_copy(constant_hbm, constant, load_sem.at[1]),
        pltpu.make_async_copy(geometry_hbm, geometry, load_sem.at[2]),
    ]
    barrier = pltpu.get_barrier_semaphore()
    for peer in halo + in_column + in_plane:
        pl.semaphore_signal(barrier, inc=1, device_id=peer, device_id_type=MESH)
    for load in loads:
        load.start()

    lane = lax.broadcasted_iota(jnp.int32, (NODES, LANES), 1)
    sub = lax.broadcasted_iota(jnp.int32, (NODES, LANES), 0)
    node = lax.rem(lane, NODES)
    from_right = (node == NODES - 1) & (lane != LANES - 1)
    from_left = (node == 0) & (lane != 0)

    def assemble(values, k):
        tiles = [[values[x, 8 * e : 8 * e + 8] for e in range(EY)] for x in range(EX * NODES)]
        for e in range(EY):
            joined = tiles[NODES - 1][e] + tiles[NODES][e]
            tiles[NODES - 1][e] = tiles[NODES][e] = joined
        for x in range(EX * NODES):
            if x == NODES:
                for e in range(EY):
                    partial[k, x, 8 * e : 8 * e + 8, :] = tiles[NODES - 1][e]
                tiles[x] = tiles[NODES - 1]
                continue
            row = tiles[x]
            new = list(row)
            for e in range(EY - 1):
                new[e] = new[e] + jnp.where(sub == 7, pltpu.roll(row[e + 1], 7, 0), 0.0)
                new[e + 1] = new[e + 1] + jnp.where(sub == 0, pltpu.roll(row[e], 1, 0), 0.0)
            new[0] = jnp.where(sub == 0, 0.0, new[0])
            new[-1] = jnp.where(sub == 7, 0.0, new[-1])
            for e in range(EY):
                t = new[e]
                t = (
                    t
                    + jnp.where(from_right, pltpu.roll(t, LANES - 1, 1), 0.0)
                    + jnp.where(from_left, pltpu.roll(t, 1, 1), 0.0)
                )
                new[e] = t
                partial[k, x, 8 * e : 8 * e + 8, :] = t
            tiles[x] = new
        pack = jnp.zeros((NODES, LANES), jnp.float32)
        for x in range(EX * NODES):
            for e in range(EY):
                j = x * EY + e
                pack = jnp.where(lane // 2 == j, pltpu.roll(tiles[x][e], 2 * j + 1, 1), pack)
        packed[k] = pack

    last = EX * NODES - 1

    def exchanges(k):
        sources = [partial.at[k, 0], partial.at[k, last]] + [packed.at[k]] * 6
        targets = [planes.at[k, 1], planes.at[k, 0]]
        targets += [packs.at[k, i] for i in (1, 0, 5, 4, 3, 2)]
        slots = [1, 0, 3, 2, 7, 6, 5, 4]
        return [
            pltpu.make_async_remote_copy(
                src_ref=a,
                dst_ref=b,
                send_sem=send_sem.at[k, i],
                recv_sem=recv_sem.at[k, slots[i]],
                device_id=peer,
                device_id_type=MESH,
            )
            for i, (a, b, peer) in enumerate(zip(sources, targets, halo))
        ]

    def finish(k, want_norm):
        edge = EY * 2 * last
        low, high = lane < 2 * EY, (lane >= edge) & (lane < edge + 2 * EY)

        def with_corners(face, below, above):
            return (
                face
                + jnp.where(low, pltpu.roll(below, LANES - edge, 1), 0.0)
                + jnp.where(high, pltpu.roll(above, edge, 1), 0.0)
            )

        minus = with_corners(packs[k, 0], packs[k, 2], packs[k, 4])
        plus = with_corners(packs[k, 1], packs[k, 3], packs[k, 5])
        faces = jnp.where(
            lax.rem(lane, 2) == 0, pltpu.roll(plus, LANES - 1, 1), pltpu.roll(minus, 1, 1)
        )
        ends = (lane == 0) | (lane == LANES - 1)
        inner = jnp.zeros((NODES, LANES), jnp.float32)
        outer = jnp.zeros((NODES, LANES), jnp.float32)
        for x in range(EX * NODES):
            for e in range(EY):
                j = x * EY + e
                t = partial[k, x, 8 * e : 8 * e + 8, :]
                if x == 0:
                    t = t + planes[k, 0, 8 * e : 8 * e + 8, :]
                if x == last:
                    t = t + planes[k, 1, 8 * e : 8 * e + 8, :]
                t = t + jnp.where(ends, pltpu.roll(faces, LANES - 2 * j - 1, 1), 0.0)
                fields[k, x, 8 * e : 8 * e + 8, :] = t
                if want_norm:
                    if x % NODES in (0, NODES - 1):
                        outer = outer + t * t
                    else:
                        inner = inner + t * t
        return (inner + 0.5 * outer) * constant[2 * LANES + NODES : 2 * LANES + 2 * NODES, :]

    def fluxes(k):
        values = fields[k]
        flat = values.reshape(EX * NODES * EY * NODES, LANES)
        grad2[...] = jnp.dot(
            flat, constant[LANES : 2 * LANES, :], precision=HIGHEST
        ).reshape(values.shape)
        for r in range(3):
            grad1[16 * r : 16 * r + 16] = jnp.dot(
                constant[0:LANES, :], flat[LANES * r : LANES * r + LANES], precision=HIGHEST
            ).reshape(16, NODES, LANES)
        energy = jnp.zeros((NODES, LANES), jnp.float32)
        flux0 = {}
        for ex in range(EX):
            for e in range(EY):
                rows = slice(8 * e, 8 * e + 8)
                g0 = along_x([fields[k, ex * 8 + i, rows, :] for i in range(8)], DERIVATIVE)
                for i in range(8):
                    x = ex * 8 + i
                    j = x * EY + e
                    m = [metric[c, x, rows, :] for c in range(6)]
                    g1, g2 = grad1[j], grad2[x, rows, :]
                    f0 = m[0] * g0[i] + m[3] * g1 + m[4] * g2
                    f1 = m[3] * g0[i] + m[1] * g1 + m[5] * g2
                    f2 = m[4] * g0[i] + m[5] * g1 + m[2] * g2
                    energy = energy + (f0 * g0[i] + f1 * g1 + f2 * g2)
                    flux0[x, e] = f0
                    grad1[j] = f1
                    grad2[x, rows, :] = f2
        return flux0, energy

    def divergence(flux0):
        along2 = jnp.dot(
            grad2[...].reshape(EX * NODES * EY * NODES, LANES),
            constant[0:LANES, :],
            precision=HIGHEST,
        ).reshape(EX * NODES, EY * NODES, LANES)
        for r in range(3):
            grad1[16 * r : 16 * r + 16] = jnp.dot(
                constant[LANES : 2 * LANES, :],
                grad1[16 * r : 16 * r + 16].reshape(LANES, LANES),
                precision=HIGHEST,
            ).reshape(16, NODES, LANES)
        total = {}
        for ex in range(EX):
            for e in range(EY):
                back = along_x([flux0[ex * 8 + i, e] for i in range(8)], DERIVATIVE.T)
                for i in range(8):
                    x = ex * 8 + i
                    total[x, e] = (
                        back[i] + grad1[x * EY + e] + along2[x, 8 * e : 8 * e + 8]
                    )
        return jnp.stack(
            [
                jnp.concatenate([total[x, e] for e in range(EY)], axis=0)
                for x in range(EX * NODES)
            ]
        )

    def fold(tile, width):
        shift = LANES // 2
        while shift >= width:
            tile = tile + pltpu.roll(tile, shift, 1)
            shift //= 2
        return tile

    loads[0].wait()
    assemble(source[...], 0)
    pl.semaphore_wait(barrier, len(halo) + len(in_column) + len(in_plane))
    flight = exchanges(0)
    for copy in flight:
        copy.start()
    loads[1].wait()
    loads[2].wait()
    weight = constant[2 * LANES : 2 * LANES + NODES, :]
    for c in range(6):
        for x in range(EX * NODES):
            scaled = geometry[c, x].astype(jnp.float32)
            for e in range(EY):
                metric[c, x, 8 * e : 8 * e + 8, :] = scaled[8 * e : 8 * e + 8] * (
                    weight * float(WEIGHTS[x % NODES])
                )

    moments = []
    for k in range(ROUNDS - 1):
        for copy in flight:
            copy.wait_recv()
        moments.append(finish(k, True))
        flux0, energy = fluxes(k)
        moments.append(energy)
        if k == ROUNDS - 2:
            packed_moments = jnp.where(
                lane < 96, fold(moments[4], 32), fold(moments[5], 32)
            )
            for i in range(4):
                packed_moments = jnp.where(
                    lane // 16 == i, fold(moments[i], 16), packed_moments
                )
            row1[...] = jnp.sum(packed_moments, axis=0, keepdims=True)
            for i, peer in enumerate(in_column):
                pltpu.make_async_remote_copy(
                    src_ref=row1,
                    dst_ref=column.at[pl.ds(i, 1)],
                    send_sem=sum_send.at[0],
                    recv_sem=sum_recv.at[0],
                    device_id=peer,
                    device_id_type=MESH,
                ).start()
        for copy in flight:
            copy.wait_send()
        assemble(divergence(flux0), k + 1)
        flight = exchanges(k + 1)
        for copy in flight:
            copy.start()

    def whole(buffer, i, peer):
        return pltpu.make_async_remote_copy(
            src_ref=buffer,
            dst_ref=buffer,
            send_sem=sum_send.at[i],
            recv_sem=sum_recv.at[i],
            device_id=peer,
            device_id_type=MESH,
        )

    whole(column, 0, in_column[0]).wait_recv()
    row2[...] = row1[...] + jnp.sum(column[...], axis=0, keepdims=True)
    for i, peer in enumerate(in_plane):
        pltpu.make_async_remote_copy(
            src_ref=row2,
            dst_ref=plane.at[pl.ds(i, 1)],
            send_sem=sum_send.at[1],
            recv_sem=sum_recv.at[1],
            device_id=peer,
            device_id_type=MESH,
        ).start()
    for copy in flight:
        copy.wait_recv()
    finish(ROUNDS - 1, False)
    whole(plane, 1, in_plane[0]).wait_recv()
    total = row2[...] + jnp.sum(plane[...], axis=0, keepdims=True)
    group = lax.broadcasted_iota(jnp.int32, (1, LANES), 1)
    bounds = [0, 16, 32, 48, 64, 96, 128]
    m = [
        jnp.sum(
            jnp.where((group >= bounds[i]) & (group < bounds[i + 1]), total, 0.0),
            axis=1,
            keepdims=True,
        )
        for i in range(6)
    ]
    alpha0 = m[0] / m[1]
    norm1 = alpha0 * alpha0 * m[2] - m[0]
    beta0 = norm1 / m[0]
    q = 1.0 + beta0
    alpha1 = norm1 / (q * q * m[1] - 2.0 * q * alpha0 * m[2] + alpha0 * alpha0 * m[3])
    r1, r2 = -(alpha0 + alpha1 * q), alpha0 * alpha1
    norm2 = (
        m[0]
        + 2.0 * r1 * m[1]
        + (r1 * r1 + 2.0 * r2) * m[2]
        + 2.0 * r1 * r2 * m[3]
        + r2 * r2 * m[4]
    )
    beta1 = norm2 / norm1
    d0, d1, d2 = 1.0 + beta1 * q, r1 - beta1 * alpha0, r2
    alpha2 = norm2 / (
        d0 * d0 * m[1]
        + 2.0 * d0 * d1 * m[2]
        + (d1 * d1 + 2.0 * d0 * d2) * m[3]
        + 2.0 * d1 * d2 * m[4]
        + d2 * d2 * m[5]
    )
    x0 = alpha0 + alpha1 * q + alpha2 * d0
    x1 = alpha2 * d1 - alpha1 * alpha0
    x2 = alpha2 * d2
    coefficients = [jnp.broadcast_to(v, (NODES, LANES)) for v in (x0, x1, x2)]
    for x in range(EX * NODES):
        for e in range(EY):
            rows = slice(8 * e, 8 * e + 8)
            v = [fields[k, x, rows, :] for k in range(ROUNDS)]
            solution_ref[x, rows, :] = (
                coefficients[0] * v[0] + coefficients[1] * v[1] + coefficients[2] * v[2]
            )
            residual_ref[x, rows, :] = v[0] - (
                coefficients[0] * v[1] + coefficients[1] * v[2] + coefficients[2] * v[3]
            )
    for copy in flight:
        copy.wait_send()
    whole(column, 0, in_column[0]).wait_send()
    whole(plane, 1, in_plane[0]).wait_send()


def solution(mesh):
    count_s, count_p = mesh.shape["stream"], mesh.shape["span"]

    def step(source, geometry):
        block = (EX * NODES, EY * NODES, LANES)
        anywhere = pl.BlockSpec(memory_space=pl.ANY)
        f32 = jnp.float32
        return pl.pallas_call(
            functools.partial(kernel, count_s, count_p),
            out_shape=[jax.ShapeDtypeStruct(block, f32)] * 2,
            in_specs=[anywhere] * 3,
            out_specs=[pl.BlockSpec(memory_space=pltpu.VMEM)] * 2,
            scratch_shapes=[
                pltpu.VMEM(block, f32),
                pltpu.VMEM((6,) + block, jnp.bfloat16),
                pltpu.VMEM((2 * LANES + 2 * NODES, LANES), f32),
                pltpu.VMEM((6,) + block, f32),
                pltpu.VMEM((ROUNDS,) + block, f32),
                pltpu.VMEM((ROUNDS,) + block, f32),
                pltpu.VMEM((ROUNDS, 2) + block[1:], f32),
                pltpu.VMEM((ROUNDS, 6, NODES, LANES), f32),
                pltpu.VMEM((ROUNDS, NODES, LANES), f32),
                pltpu.VMEM((EX * NODES * EY, NODES, LANES), f32),
                pltpu.VMEM(block, f32),
                pltpu.VMEM((1, LANES), f32),
                pltpu.VMEM((1, LANES), f32),
                pltpu.VMEM((Z * CORES - 1, LANES), f32),
                pltpu.VMEM((X * Y - 1, LANES), f32),
                pltpu.SemaphoreType.DMA((3,)),
                pltpu.SemaphoreType.DMA((ROUNDS, 8)),
                pltpu.SemaphoreType.DMA((ROUNDS, 8)),
                pltpu.SemaphoreType.DMA((2,)),
                pltpu.SemaphoreType.DMA((2,)),
            ],
            compiler_params=pltpu.CompilerParams(
                collective_id=0, has_side_effects=True, vmem_limit_bytes=48 * 1024 * 1024
            ),
        )(source, geometry, jnp.asarray(constants()))

    return jax.shard_map(
        step,
        mesh=mesh,
        in_specs=(P("stream", None, "span"), P(None, "stream", None, "span")),
        out_specs=(P("stream", None, "span"), P("stream", None, "span")),
        check_vma=False,
    )
```

time: 557 us -> 63.1 us (0.11)
  blocking collectives: 352 us -> 0 us
  starting transfers between devices: 70.2 us -> 0 us
  Pallas kernels: 0 us -> 58 us
  local copies, waits for them, and re-layouts: 54.8 us -> 4.25 us
  other arithmetic: 35.8 us -> 0 us
  matrix products: 15.8 us -> 0 us
  waiting for transfers between devices: 15.7 us -> 0 us
  between operations: 11.4 us -> 0.65 us
    psum x3 -> x0, blocking collectives: 352 us -> none  [two_products(): lax.psum((jnp.sum(current * current * half_parts), jnp.sum(current * appl...]
    ppermute x16 -> x0, starting transfers between devices: 70.2 us -> none  [the longest x8 50.1 us: padded_2(): lax.ppermute(head, axis, [((i + 1) % count, i) for i in range(count)])]
    pallas_call x0 -> x1, Pallas kernels: none -> 58 us  [step(): pl.pallas_call(functools.partial(kernel, count_s, count_p), out_shape=[ja...]
    reshape x10 -> x0, local copies, waits for them, and re-layouts: 19.4 us -> none  [pair_faces(): return joined.reshape(extent)]
    dot_general x18 -> x0, matrix products: 15.8 us -> none  [the longest x6 6.85 us: derivative_lead(): jnp.einsum('ij,xejz->xeiz', matrix, blocks, precision=lax.Precision.HIGHEST)]
    ppermute x16 -> x0, waiting for transfers between devices: 15.7 us -> none  [the longest x8 12.2 us: padded_2(): lax.ppermute(tail, axis, [(i, (i + 1) % count) for i in range(count)])]
    reduce_sum x3 -> x0, other arithmetic: 10.6 us -> none  [two_products(): jnp.sum(current * applied * half_parts)]
    concatenate x7 -> x0, local copies, waits for them, and re-layouts: 8.76 us -> none  [the longest x4 8.18 us: pair_faces(): jnp.concatenate([jnp.expand_dims(prev_planes, axis_dim + 1), middle, jnp....]
  transfers between devices with their start and end apart: 16 -> 0, of which waited for: 8 -> 0; matrix products, arithmetic and copies ran while one was open for 2% -> 0% of each run, Pallas kernels for 0% -> 0%
where the time goes in v1:
time: 63.1 us; the launch traced here: 62.9 us
  Pallas kernels  58 us (92%)
  local copies, waits for them, and re-layouts  4.25 us (7%)
  between operations  0.65 us (1%)
    pallas_call x1, Pallas kernels, step(): pl.pallas_call(functools.partial(kernel, count_s, count_p), out_shape=[ja...  58 us
    unnamed x8, local copies, waits for them, and re-layouts  4.25 us

profile of v1, /device:TPU:1, one launch (start us, length us, event | category | flops | bytes accessed | tf_op | source)
XLA Modules:
  0.0 62.9 jit_solution(521266270543648376)
XLA Ops:
  0.6 0.0 copy-start
  0.6 1.1 %copy-done = bf16[6,16,24,128]{3,2,1,0:T(8,128)(2,1)S(1)} copy-done((bf16[6,16,24,128]{3,2,1,0:T(8,128)(2,1)S(1)}, bf16[6,16,24,128]{3,2,1,0:T(8,128)(2,1)}, u32[]{:S(2)}) %copy-start) | copy-done | bytes 589848
  1.7 0.0 copy-start.1
  1.7 0.9 %copy-done.1 = f32[16,24,128]{2,1,0:T(8,128)S(1)} copy-done((f32[16,24,128]{2,1,0:T(8,128)S(1)}, f32[16,24,128]{2,1,0:T(8,128)}, u32[]{:S(2)}) %copy-start.1) | copy-done | bytes 196632
  2.6 0.0 copy-start.2
  2.6 0.9 %copy-done.2 = f32[272,128]{1,0:T(8,128)S(1)} copy-done((f32[272,128]{1,0:T(8,128)S(1)}, f32[272,128]{1,0:T(8,128)}, u32[]{:S(2)}) %copy-start.2) | copy-done | bytes 139288
  3.5 58.0 %shard_map.50 = (f32[16,24,128]{2,1,0:T(8,128)S(1)}, f32[16,24,128]{2,1,0:T(8,128)S(1)}) custom-call(f32[16,24,128]{2,1,0:T(8,128)S(1)} %copy-done.1, bf16[6,16,24,128]{3,2,1,0:T(8,128)(2,1)S(1)} %copy-done, f32[272,128]{1,0:T(8,128)S(1)} %copy-done.2), custom_call_target="tpu_custom_call" | custom-call | tf_op jit(solution)/shard_map/pallas_call | solution.py:460
  61.6 0.7 %copy.7 = f32[16,24,128]{2,1,0:T(8,128)} copy(f32[16,24,128]{2,1,0:T(8,128)S(1)} %get-tuple-element.4) | data formatting | bytes 393216
  62.2 0.7 %copy.8 = f32[16,24,128]{2,1,0:T(8,128)} copy(f32[16,24,128]{2,1,0:T(8,128)S(1)} %get-tuple-element.5) | data formatting | bytes 393216
Async XLA Ops:
  0.6 1.1 %copy-start = (bf16[6,16,24,128]{3,2,1,0:T(8,128)(2,1)S(1)}, bf16[6,16,24,128]{3,2,1,0:T(8,128)(2,1)}, u32[]{:S(2)}) copy-start(bf16[6,16,24,128]{3,2,1,0:T(8,128)(2,1)} %geometry_hbm.1) | copy-start | bytes 1769476
  1.7 0.9 %copy-start.1 = (f32[16,24,128]{2,1,0:T(8,128)S(1)}, f32[16,24,128]{2,1,0:T(8,128)}, u32[]{:S(2)}) copy-start(f32[16,24,128]{2,1,0:T(8,128)} %source_hbm.1) | copy-start | bytes 589828
  2.6 0.9 %copy-start.2 = (f32[272,128]{1,0:T(8,128)S(1)}, f32[272,128]{1,0:T(8,128)}, u32[]{:S(2)}) copy-start(f32[272,128]{1,0:T(8,128)} %constant.2.clone.constant_hbm) | copy-start | bytes 417796

commit v2 on v1

--- a/solution.py
+++ b/solution.py
@@ -14,9 +14,11 @@
 EY = 3
 LANES = 128
 ROUNDS = 4
-HIGHEST = lax.Precision.HIGHEST
+ROWS = EX * NODES * EY * NODES
 Z_HI, X, Y, CORES, Z_LO = 3, 4, 8, 2, 4
 Z = Z_HI * Z_LO
+HEADS = 2
+FANOUT = (Z - HEADS) // HEADS
 
 
 def gll_tables():
@@ -67,10 +69,48 @@
     half = np.ones(NODES)
     half[0] = half[-1] = 0.5
     copies = LANES // NODES
-    blocks = np.kron(np.eye(copies), DERIVATIVE)
     weight = WEIGHTS[:, None] * np.tile(WEIGHTS, copies)[None, :]
     halves = half[:, None] * np.tile(half, copies)[None, :]
-    return np.concatenate([blocks, blocks.T, weight, halves]).astype(np.float32)
+    return np.concatenate([weight, halves]).astype(np.float32)
+
+
+def matrices():
+    blocks = np.kron(np.eye(LANES // NODES), DERIVATIVE).astype(np.float32)
+    parts = []
+    for matrix in (blocks, blocks.T):
+        lead = matrix.astype(jnp.bfloat16)
+        parts += [lead, (matrix - lead.astype(np.float32)).astype(jnp.bfloat16)]
+    return np.stack(parts)
+
+
+def split(values):
+    lead = values.astype(jnp.bfloat16)
+    return lead, (values - lead.astype(jnp.float32)).astype(jnp.bfloat16)
+
+
+def along_z(parts, matrix):
+    wide = jnp.concatenate([matrix[0], matrix[1]], axis=1)
+    product = jnp.dot(
+        jnp.concatenate(parts, axis=1),
+        jnp.concatenate([wide, wide], axis=0),
+        preferred_element_type=jnp.float32,
+    )
+    return product[:, :LANES] + product[:, LANES:]
+
+
+def along_y(parts, matrix):
+    tall = jnp.concatenate([matrix[0], matrix[1]], axis=0)
+    stacked = [
+        jnp.concatenate([part[LANES * r : LANES * r + LANES] for part in parts], axis=0)
+        for r in range(ROWS // LANES)
+    ]
+    product = jnp.dot(
+        jnp.concatenate([tall, tall], axis=1),
+        jnp.concatenate(stacked, axis=1),
+        preferred_element_type=jnp.float32,
+    )
+    product = product[:LANES] + product[LANES:]
+    return [product[:, LANES * r : LANES * r + LANES] for r in range(ROWS // LANES)]
 
 
 def neighbours(count_s, count_p):
@@ -80,18 +120,14 @@
     return s, p, down, up, left, right
 
 
-def column_peers(s, p):
-    core, z_hi = lax.rem(s, CORES), s // (X * Y * CORES)
-    base = s - core - z_hi * (X * Y * CORES)
-    z = z_hi * Z_LO + p
-    peers = []
-    for dz in range(Z):
-        for dc in range(CORES):
-            if dz or dc:
-                other = lax.rem(z + dz, Z)
-                c = lax.rem(core + dc, CORES)
-                peers.append((base + (other // Z_LO) * (X * Y * CORES) + c, lax.rem(other, Z_LO)))
-    return peers
+def place(s, p):
+    core, row = lax.rem(s, CORES), s // CORES
+    y, x, z_hi = lax.rem(row, Y), lax.rem(row // Y, X), row // (X * Y)
+    return core, x, y, z_hi * Z_LO + p, (x * Y + y) * CORES
+
+
+def in_column(base, z, core):
+    return base + (z // Z_LO) * (X * Y * CORES) + core, lax.rem(z, Z_LO)
 
 
 def plane_peers(s, p):
@@ -123,11 +159,13 @@
     source_hbm,
     geometry_hbm,
     constant_hbm,
+    matrix_hbm,
     solution_ref,
     residual_ref,
     source,
     geometry,
     constant,
+    matrix,
     metric,
     fields,
     partial,
@@ -138,6 +176,7 @@
     grad2,
     row1,
     row2,
+    result,
     column,
     plane,
     load_sem,
@@ -147,20 +186,36 @@
     sum_recv,
 ):
     s, p, down, up, left, right = neighbours(count_s, count_p)
+    core, _, _, z, base = place(s, p)
+    gathers = z < HEADS
     halo = [(down, p), (up, p), (s, left), (s, right)]
     halo += [(down, left), (down, right), (up, left), (up, right)]
-    in_column, in_plane = column_peers(s, p), plane_peers(s, p)
+    in_plane = plane_peers(s, p)
+    heads = [(h, c) for h in range(HEADS) for c in range(CORES)]
+    below = [
+        in_column(base, lax.rem(z + dz, Z), lax.rem(core + dc, CORES))
+        for dz in range(Z)
+        for dc in range(CORES)
+        if dz or dc
+    ]
 
     loads = [
         pltpu.make_async_copy(source_hbm, source, load_sem.at[0]),
         pltpu.make_async_copy(constant_hbm, constant, load_sem.at[1]),
         pltpu.make_async_copy(geometry_hbm, geometry, load_sem.at[2]),
+        pltpu.make_async_copy(matrix_hbm, matrix, load_sem.at[3]),
     ]
     barrier = pltpu.get_barrier_semaphore()
-    for peer in halo + in_column + in_plane:
+    for peer in halo:
         pl.semaphore_signal(barrier, inc=1, device_id=peer, device_id_type=MESH)
     for load in loads:
         load.start()
+
+    @pl.when(gathers)
+    def _():
+        for peer in in_plane + below:
+            pl.semaphore_signal(barrier, inc=1, device_id=peer, device_id_type=MESH)
+
 
     lane = lax.broadcasted_iota(jnp.int32, (NODES, LANES), 1)
     sub = lax.broadcasted_iota(jnp.int32, (NODES, LANES), 0)
@@ -256,18 +311,14 @@
                         outer = outer + t * t
                     else:
                         inner = inner + t * t
-        return (inner + 0.5 * outer) * constant[2 * LANES + NODES : 2 * LANES + 2 * NODES, :]
+        return (inner + 0.5 * outer) * constant[NODES : 2 * NODES, :]
 
     def fluxes(k):
         values = fields[k]
-        flat = values.reshape(EX * NODES * EY * NODES, LANES)
-        grad2[...] = jnp.dot(
-            flat, constant[LANES : 2 * LANES, :], precision=HIGHEST
-        ).reshape(values.shape)
-        for r in range(3):
-            grad1[16 * r : 16 * r + 16] = jnp.dot(
-                constant[0:LANES, :], flat[LANES * r : LANES * r + LANES], precision=HIGHEST
-            ).reshape(16, NODES, LANES)
+        parts = split(values.reshape(ROWS, LANES))
+        grad2[...] = along_z(parts, (matrix[2], matrix[3])).reshape(values.shape)
+        for r, group in enumerate(along_y(parts, (matrix[0], matrix[1]))):
+            grad1[16 * r : 16 * r + 16] = group.reshape(16, NODES, LANES)
         energy = jnp.zeros((NODES, LANES), jnp.float32)
         flux0 = {}
         for ex in range(EX):
@@ -289,17 +340,11 @@
         return flux0, energy
 
     def divergence(flux0):
-        along2 = jnp.dot(
-            grad2[...].reshape(EX * NODES * EY * NODES, LANES),
-            constant[0:LANES, :],
-            precision=HIGHEST,
-        ).reshape(EX * NODES, EY * NODES, LANES)
-        for r in range(3):
-            grad1[16 * r : 16 * r + 16] = jnp.dot(
-                constant[LANES : 2 * LANES, :],
-                grad1[16 * r : 16 * r + 16].reshape(LANES, LANES),
-                precision=HIGHEST,
-            ).reshape(16, NODES, LANES)
+        flat = split(grad2[...].reshape(ROWS, LANES))
+        along2 = along_z(flat, (matrix[0], matrix[1])).reshape(EX * NODES, EY * NODES, LANES)
+        flat = split(grad1[...].reshape(ROWS, LANES))
+        for r, group in enumerate(along_y(flat, (matrix[2], matrix[3]))):
+            grad1[16 * r : 16 * r + 16] = group.reshape(16, NODES, LANES)
         total = {}
         for ex in range(EX):
             for e in range(EY):
@@ -325,13 +370,17 @@
 
     loads[0].wait()
     assemble(source[...], 0)
-    pl.semaphore_wait(barrier, len(halo) + len(in_column) + len(in_plane))
+    pl.semaphore_wait(
+        barrier,
+        len(halo) + len(heads) + jnp.where(gathers, len(in_plane) - 1, 0),
+    )
     flight = exchanges(0)
     for copy in flight:
         copy.start()
     loads[1].wait()
     loads[2].wait()
-    weight = constant[2 * LANES : 2 * LANES + NODES, :]
+    loads[3].wait()
+    weight = constant[0:NODES, :]
     for c in range(6):
         for x in range(EX * NODES):
             scaled = geometry[c, x].astype(jnp.float32)
@@ -356,15 +405,20 @@
                     lane // 16 == i, fold(moments[i], 16), packed_moments
                 )
             row1[...] = jnp.sum(packed_moments, axis=0, keepdims=True)
-            for i, peer in enumerate(in_column):
-                pltpu.make_async_remote_copy(
-                    src_ref=row1,
-                    dst_ref=column.at[pl.ds(i, 1)],
-                    send_sem=sum_send.at[0],
-                    recv_sem=sum_recv.at[0],
-                    device_id=peer,
-                    device_id_type=MESH,
-                ).start()
+            for head, c in heads:
+                offset = lax.rem(z + Z - head, Z) * CORES + lax.rem(core + CORES - c, CORES)
+
+                @pl.when(offset > 0)
+                def _(head=head, c=c, offset=offset):
+                    pltpu.make_async_remote_copy(
+                        src_ref=row1,
+                        dst_ref=column.at[offset - 1],
+                        send_sem=sum_send.at[0],
+                        recv_sem=sum_recv.at[0],
+                        device_id=in_column(base, jnp.int32(head), c),
+                        device_id_type=MESH,
+                    ).start()
+
         for copy in flight:
             copy.wait_send()
         assemble(divergence(flux0), k + 1)
@@ -372,32 +426,54 @@
         for copy in flight:
             copy.start()
 
-    def whole(buffer, i, peer):
+    def whole(buffer, i):
         return pltpu.make_async_remote_copy(
             src_ref=buffer,
             dst_ref=buffer,
             send_sem=sum_send.at[i],
             recv_sem=sum_recv.at[i],
-            device_id=peer,
+            device_id=halo[0],
             device_id_type=MESH,
         )
 
-    whole(column, 0, in_column[0]).wait_recv()
-    row2[...] = row1[...] + jnp.sum(column[...], axis=0, keepdims=True)
-    for i, peer in enumerate(in_plane):
-        pltpu.make_async_remote_copy(
-            src_ref=row2,
-            dst_ref=plane.at[pl.ds(i, 1)],
-            send_sem=sum_send.at[1],
-            recv_sem=sum_recv.at[1],
-            device_id=peer,
-            device_id_type=MESH,
-        ).start()
+    @pl.when(gathers)
+    def _():
+        whole(column, 0).wait_recv()
+        row2[...] = row1[...] + jnp.sum(column[...], axis=0)
+        for i, peer in enumerate(in_plane):
+            pltpu.make_async_remote_copy(
+                src_ref=row2,
+                dst_ref=plane.at[i],
+                send_sem=sum_send.at[1],
+                recv_sem=sum_recv.at[1],
+                device_id=peer,
+                device_id_type=MESH,
+            ).start()
+
     for copy in flight:
         copy.wait_recv()
     finish(ROUNDS - 1, False)
-    whole(plane, 1, in_plane[0]).wait_recv()
-    total = row2[...] + jnp.sum(plane[...], axis=0, keepdims=True)
+
+    @pl.when(gathers)
+    def _():
+        whole(plane, 1).wait_recv()
+        result[...] = row2[...] + jnp.sum(plane[...], axis=0)
+        for i in range(FANOUT):
+            target = jnp.where(z == 0, Z - 1 - i, HEADS + i)
+            pltpu.make_async_remote_copy(
+                src_ref=result,
+                dst_ref=result,
+                send_sem=sum_send.at[2],
+                recv_sem=sum_recv.at[2],
+                device_id=in_column(base, target, core),
+                device_id_type=MESH,
+            ).start()
+
+    @pl.when(jnp.logical_not(gathers))
+    def _():
+        whole(result, 2).wait_recv()
+
+    total = result[...]
     group = lax.broadcasted_iota(jnp.int32, (1, LANES), 1)
     bounds = [0, 16, 32, 48, 64, 96, 128]
     m = [
@@ -446,8 +522,16 @@
             )
     for copy in flight:
         copy.wait_send()
-    whole(column, 0, in_column[0]).wait_send()
-    whole(plane, 1, in_plane[0]).wait_send()
+
+    @pl.when(gathers)
+    def _():
+        whole(column.at[pl.ds(0, len(heads) - 1)], 0).wait_send()
+        whole(plane, 1).wait_send()
+        whole(column.at[pl.ds(0, FANOUT)], 2).wait_send()
+
+    @pl.when(jnp.logical_not(gathers))
+    def _():
+        whole(column.at[pl.ds(0, len(heads))], 0).wait_send()
 
 
 def solution(mesh):
@@ -455,17 +539,18 @@
 
     def step(source, geometry):
         block = (EX * NODES, EY * NODES, LANES)
-        anywhere = pl.BlockSpec(memory_space=pl.ANY)
+        in_hbm = pl.BlockSpec(memory_space=pltpu.HBM)
         f32 = jnp.float32
         return pl.pallas_call(
             functools.partial(kernel, count_s, count_p),
-            out_shape=[jax.ShapeDtypeStruct(block, f32)] * 2,
-            in_specs=[anywhere] * 3,
+            out_shape=[pltpu.VMEM(block, f32)] * 2,
+            in_specs=[in_hbm] * 4,
             out_specs=[pl.BlockSpec(memory_space=pltpu.VMEM)] * 2,
             scratch_shapes=[
                 pltpu.VMEM(block, f32),
                 pltpu.VMEM((6,) + block, jnp.bfloat16),
-                pltpu.VMEM((2 * LANES + 2 * NODES, LANES), f32),
+                pltpu.VMEM((2 * NODES, LANES), f32),
+                pltpu.VMEM((4, LANES, LANES), jnp.bfloat16),
                 pltpu.VMEM((6,) + block, f32),
                 pltpu.VMEM((ROUNDS,) + block, f32),
                 pltpu.VMEM((ROUNDS,) + block, f32),
@@ -476,18 +561,19 @@
                 pltpu.VMEM(block, f32),
                 pltpu.VMEM((1, LANES), f32),
                 pltpu.VMEM((1, LANES), f32),
-                pltpu.VMEM((Z * CORES - 1, LANES), f32),
-                pltpu.VMEM((X * Y - 1, LANES), f32),
-                pltpu.SemaphoreType.DMA((3,)),
+                pltpu.VMEM((1, LANES), f32),
+                pltpu.VMEM((Z * CORES - 1, 1, LANES), f32),
+                pltpu.VMEM((X * Y - 1, 1, LANES), f32),
+                pltpu.SemaphoreType.DMA((4,)),
                 pltpu.SemaphoreType.DMA((ROUNDS, 8)),
                 pltpu.SemaphoreType.DMA((ROUNDS, 8)),
-                pltpu.SemaphoreType.DMA((2,)),
-                pltpu.SemaphoreType.DMA((2,)),
+                pltpu.SemaphoreType.DMA((3,)),
+                pltpu.SemaphoreType.DMA((3,)),
             ],
             compiler_params=pltpu.CompilerParams(
                 collective_id=0, has_side_effects=True, vmem_limit_bytes=48 * 1024 * 1024
             ),
-        )(source, geometry, jnp.asarray(constants()))
+        )(*(pltpu.with_memory_space_constraint(v, pltpu.HBM) for v in (source, geometry, jnp.asarray(constants()), jnp.asarray(matrices()))))
 
     return jax.shard_map(
         step,

time: 63.1 us -> 56.8 us (0.900)
  Pallas kernels: 58 us -> 54.1 us
  local copies, waits for them, and re-layouts: 4.25 us -> 1.36 us
    pallas_call x1, Pallas kernels: 58 us -> 54.1 us  [step(): pl.pallas_call(functools.partial(kernel, count_s, count_p), out_shape=[pl...]
    unnamed x8 -> x2, local copies, waits for them, and re-layouts: 4.25 us -> 1.36 us
where the time goes in v2:
time: 56.8 us; the launch traced here: 56.1 us
  Pallas kernels  54.1 us (95%)
  local copies, waits for them, and re-layouts  1.36 us (2%)
  between operations  0.64 us (1%)
    pallas_call x1, Pallas kernels, step(): pl.pallas_call(functools.partial(kernel, count_s, count_p), out_shape=[pl...  54.1 us
    unnamed x2, local copies, waits for them, and re-layouts  1.36 us

profile of v2, /device:TPU:1, one launch (start us, length us, event | category | flops | bytes accessed | tf_op | source)
XLA Modules:
  0.0 56.1 jit_solution(12102785397267557991)
XLA Ops:
  0.6 54.1 %shard_map.59 = (f32[16,24,128]{2,1,0:T(8,128)S(1)}, f32[16,24,128]{2,1,0:T(8,128)S(1)}) custom-call(f32[16,24,128]{2,1,0:T(8,128)} %source_hbm.1, bf16[6,16,24,128]{3,2,1,0:T(8,128)(2,1)} %geometry_hbm.1, f32[16,128]{1,0:T(8,128)} %constant.4.clone.constant_hbm, bf16[4,128,128]{2,1,0:T(8,128)(2,1)} %constant.5.clone.matrix_hbm), custom_call_target="tpu_custom_call" | custom-call | tf_op jit(solution)/shard_map/pallas_call | solution.py:544
  54.7 0.7 %copy.8 = f32[16,24,128]{2,1,0:T(8,128)} copy(f32[16,24,128]{2,1,0:T(8,128)S(1)} %get-tuple-element.2) | data formatting | bytes 393216
  55.4 0.7 %copy.9 = f32[16,24,128]{2,1,0:T(8,128)} copy(f32[16,24,128]{2,1,0:T(8,128)S(1)} %get-tuple-element.3) | data formatting | bytes 393216

commit v3 on v2

--- a/solution.py
+++ b/solution.py
@@ -99,10 +99,11 @@
 
 
 def along_y(parts, matrix):
+    groups = parts[0].shape[0] // LANES
     tall = jnp.concatenate([matrix[0], matrix[1]], axis=0)
     stacked = [
         jnp.concatenate([part[LANES * r : LANES * r + LANES] for part in parts], axis=0)
-        for r in range(ROWS // LANES)
+        for r in range(groups)
     ]
     product = jnp.dot(
         jnp.concatenate([tall, tall], axis=1),
@@ -110,7 +111,7 @@
         preferred_element_type=jnp.float32,
     )
     product = product[:LANES] + product[LANES:]
-    return [product[:, LANES * r : LANES * r + LANES] for r in range(ROWS // LANES)]
+    return [product[:, LANES * r : LANES * r + LANES] for r in range(groups)]
 
 
 def neighbours(count_s, count_p):
@@ -172,6 +173,12 @@
     planes,
     packs,
     packed,
+    early,
+    early_pack,
+    own_side,
+    far_side,
+    face,
+    response,
     grad1,
     grad2,
     row1,
@@ -184,10 +191,15 @@
     recv_sem,
     sum_send,
     sum_recv,
+    side_sem,
 ):
     s, p, down, up, left, right = neighbours(count_s, count_p)
     core, _, _, z, base = place(s, p)
     gathers = z < HEADS
+    block = X * Y * CORES
+    long_down = lax.rem(s, block) == 0
+    long_up = lax.rem(s, block) == block - 1
+    is_long = long_down | long_up
     halo = [(down, p), (up, p), (s, left), (s, right)]
     halo += [(down, left), (down, right), (up, left), (up, right)]
     in_plane = plane_peers(s, p)
@@ -223,7 +235,7 @@
     from_right = (node == NODES - 1) & (lane != LANES - 1)
     from_left = (node == 0) & (lane != 0)
 
-    def assemble(values, k):
+    def assemble(values, sums, pack_ref):
         tiles = [[values[x, 8 * e : 8 * e + 8] for e in range(EY)] for x in range(EX * NODES)]
         for e in range(EY):
             joined = tiles[NODES - 1][e] + tiles[NODES][e]
@@ -231,7 +243,7 @@
         for x in range(EX * NODES):
             if x == NODES:
                 for e in range(EY):
-                    partial[k, x, 8 * e : 8 * e + 8, :] = tiles[NODES - 1][e]
+                    sums[x, 8 * e : 8 * e + 8, :] = tiles[NODES - 1][e]
                 tiles[x] = tiles[NODES - 1]
                 continue
             row = tiles[x]
@@ -249,19 +261,21 @@
                     + jnp.where(from_left, pltpu.roll(t, 1, 1), 0.0)
                 )
                 new[e] = t
-                partial[k, x, 8 * e : 8 * e + 8, :] = t
+                sums[x, 8 * e : 8 * e + 8, :] = t
             tiles[x] = new
         pack = jnp.zeros((NODES, LANES), jnp.float32)
         for x in range(EX * NODES):
             for e in range(EY):
                 j = x * EY + e
                 pack = jnp.where(lane // 2 == j, pltpu.roll(tiles[x][e], 2 * j + 1, 1), pack)
-        packed[k] = pack
+        pack_ref[...] = pack
 
     last = EX * NODES - 1
 
-    def exchanges(k):
-        sources = [partial.at[k, 0], partial.at[k, last]] + [packed.at[k]] * 6
+    def exchanges(k, sums=None, pack_ref=None):
+        sums = partial.at[k] if sums is None else sums
+        pack_ref = packed.at[k] if pack_ref is None else pack_ref
+        sources = [sums.at[0], sums.at[last]] + [pack_ref] * 6
         targets = [planes.at[k, 1], planes.at[k, 0]]
         targets += [packs.at[k, i] for i in (1, 0, 5, 4, 3, 2)]
         slots = [1, 0, 3, 2, 7, 6, 5, 4]
@@ -277,19 +291,19 @@
             for i, (a, b, peer) in enumerate(zip(sources, targets, halo))
         ]
 
-    def finish(k, want_norm):
+    def finish(k, want_norm, with_down=True, with_up=True):
         edge = EY * 2 * last
         low, high = lane < 2 * EY, (lane >= edge) & (lane < edge + 2 * EY)
 
         def with_corners(face, below, above):
-            return (
-                face
-                + jnp.where(low, pltpu.roll(below, LANES - edge, 1), 0.0)
-                + jnp.where(high, pltpu.roll(above, edge, 1), 0.0)
-            )
-
-        minus = with_corners(packs[k, 0], packs[k, 2], packs[k, 4])
-        plus = with_corners(packs[k, 1], packs[k, 3], packs[k, 5])
+            if with_down:
+                face = face + jnp.where(low, pltpu.roll(packs[k, below], LANES - edge, 1), 0.0)
+            if with_up:
+                face = face + jnp.where(high, pltpu.roll(packs[k, above], edge, 1), 0.0)
+            return face
+
+        minus = with_corners(packs[k, 0], 2, 4)
+        plus = with_corners(packs[k, 1], 3, 5)
         faces = jnp.where(
             lax.rem(lane, 2) == 0, pltpu.roll(plus, LANES - 1, 1), pltpu.roll(minus, 1, 1)
         )
@@ -300,9 +314,9 @@
             for e in range(EY):
                 j = x * EY + e
                 t = partial[k, x, 8 * e : 8 * e + 8, :]
-                if x == 0:
+                if x == 0 and with_down:
                     t = t + planes[k, 0, 8 * e : 8 * e + 8, :]
-                if x == last:
+                if x == last and with_up:
                     t = t + planes[k, 1, 8 * e : 8 * e + 8, :]
                 t = t + jnp.where(ends, pltpu.roll(faces, LANES - 2 * j - 1, 1), 0.0)
                 fields[k, x, 8 * e : 8 * e + 8, :] = t
@@ -339,7 +353,7 @@
                     grad2[x, rows, :] = f2
         return flux0, energy
 
-    def divergence(flux0):
+    def divergence(flux0, add=False):
         flat = split(grad2[...].reshape(ROWS, LANES))
         along2 = along_z(flat, (matrix[0], matrix[1])).reshape(EX * NODES, EY * NODES, LANES)
         flat = split(grad1[...].reshape(ROWS, LANES))
@@ -354,6 +368,11 @@
                     total[x, e] = (
                         back[i] + grad1[x * EY + e] + along2[x, 8 * e : 8 * e + 8]
                     )
+        if add:
+            for e in range(EY):
+                extra = response[8 * e : 8 * e + 8, :]
+                total[0, e] = total[0, e] + jnp.where(long_down, extra, 0.0)
+                total[last, e] = total[last, e] + jnp.where(long_up, extra, 0.0)
         return jnp.stack(
             [
                 jnp.concatenate([total[x, e] for e in range(EY)], axis=0)
@@ -361,6 +380,45 @@
             ]
         )
 
+    def side_copy():
+        return pltpu.make_async_remote_copy(
+            src_ref=own_side,
+            dst_ref=far_side,
+            send_sem=side_sem.at[0],
+            recv_sem=side_sem.at[1],
+            device_id=(jnp.where(long_down, down, up), p),
+            device_id_type=MESH,
+        )
+
+    def describe_side(first, plane_index):
+        squares = DERIVATIVE[:, 0 if first == 0 else NODES - 1] ** 2
+        own_side[0] = sum(metric[0, first + i] * float(squares[i]) for i in range(NODES))
+        for c in range(1, 6):
+            own_side[c] = metric[c, plane_index]
+
+    def respond():
+        values = face[...]
+        rest = jnp.zeros((LANES - EY * NODES, LANES), jnp.float32)
+        slope = jnp.where(
+            long_down, float(DERIVATIVE[NODES - 1, NODES - 1]), float(DERIVATIVE[0, 0])
+        )
+
+        def tall(v):
+            return split(jnp.concatenate([v, rest], axis=0))
+
+        parts = tall(values)
+        d1 = along_y(parts, (matrix[0], matrix[1]))[0][: EY * NODES]
+        d2 = along_z(parts, (matrix[2], matrix[3]))[: EY * NODES]
+        d0 = slope * values
+        f1 = far_side[3] * d0 + far_side[1] * d1 + far_side[5] * d2
+        f2 = far_side[4] * d0 + far_side[5] * d1 + far_side[2] * d2
+        response[...] = (
+            far_side[0] * values
+            + slope * (far_side[3] * d1 + far_side[4] * d2)
+            + along_y(tall(f1), (matrix[2], matrix[3]))[0][: EY * NODES]
+            + along_z(tall(f2), (matrix[0], matrix[1]))[: EY * NODES]
+        )
+
     def fold(tile, width):
         shift = LANES // 2
         while shift >= width:
@@ -369,7 +427,7 @@
         return tile
 
     loads[0].wait()
-    assemble(source[...], 0)
+    assemble(source[...], partial.at[0], packed.at[0])
     pl.semaphore_wait(
         barrier,
         len(halo) + len(heads) + jnp.where(gathers, len(in_plane) - 1, 0),
@@ -389,10 +447,44 @@
                     weight * float(WEIGHTS[x % NODES])
                 )
 
+    to_down, to_up = (0, 4, 5), (1, 6, 7)
+    from_down, from_up = to_up, to_down
+
+    def ahead(copies_from, copies_to, side_first, side_plane, **skip):
+        describe_side(side_first, side_plane)
+        side_copy().start()
+        for i, copy in enumerate(flight):
+            if i not in copies_from:
+                copy.wait_recv()
+        finish(0, False, **skip)
+        face[...] = fields[0, side_plane]
+        flux, _ = fluxes(0)
+        assemble(divergence(flux), early, early_pack)
+        for i, copy in enumerate(exchanges(1, early, early_pack)):
+            if i in copies_to:
+                copy.start()
+        for i, copy in enumerate(flight):
+            if i in copies_from:
+                copy.wait_recv()
+
+    @pl.when(long_down)
+    def _():
+        ahead(from_down, to_down, 0, 0, with_down=False)
+
+    @pl.when(long_up)
+    def _():
+        ahead(from_up, to_up, NODES, last, with_up=False)
+
+    @pl.when(jnp.logical_not(is_long))
+    def _():
+        for copy in flight:
+            copy.wait_recv()
+
     moments = []
     for k in range(ROUNDS - 1):
-        for copy in flight:
-            copy.wait_recv()
+        if k > 0:
+            for copy in flight:
+                copy.wait_recv()
         moments.append(finish(k, True))
         flux0, energy = fluxes(k)
         moments.append(energy)
@@ -421,10 +513,20 @@
 
         for copy in flight:
             copy.wait_send()
-        assemble(divergence(flux0), k + 1)
+        if k == 0:
+
+            @pl.when(is_long)
+            def _():
+                side_copy().wait_recv()
+                respond()
+
+        assemble(divergence(flux0, k == 0), partial.at[k + 1], packed.at[k + 1])
         flight = exchanges(k + 1)
-        for copy in flight:
-            copy.start()
+        for i, copy in enumerate(flight):
+            if k > 0 or i in (2, 3):
+                copy.start()
+            else:
+                pl.when(jnp.logical_not(long_down if i in to_down else long_up))(copy.start)
 
     def whole(buffer, i):
         return pltpu.make_async_remote_copy(
@@ -523,6 +625,10 @@
     for copy in flight:
         copy.wait_send()
 
+    @pl.when(is_long)
+    def _():
+        side_copy().wait_send()
+
     @pl.when(gathers)
     def _():
         whole(column.at[pl.ds(0, len(heads) - 1)], 0).wait_send()
@@ -557,6 +663,12 @@
                 pltpu.VMEM((ROUNDS, 2) + block[1:], f32),
                 pltpu.VMEM((ROUNDS, 6, NODES, LANES), f32),
                 pltpu.VMEM((ROUNDS, NODES, LANES), f32),
+                pltpu.VMEM(block, f32),
+                pltpu.VMEM((NODES, LANES), f32),
+                pltpu.VMEM((6,) + block[1:], f32),
+                pltpu.VMEM((6,) + block[1:], f32),
+                pltpu.VMEM(block[1:], f32),
+                pltpu.VMEM(block[1:], f32),
                 pltpu.VMEM((EX * NODES * EY, NODES, LANES), f32),
                 pltpu.VMEM(block, f32),
                 pltpu.VMEM((1, LANES), f32),
@@ -569,6 +681,7 @@
                 pltpu.SemaphoreType.DMA((ROUNDS, 8)),
                 pltpu.SemaphoreType.DMA((3,)),
                 pltpu.SemaphoreType.DMA((3,)),
+                pltpu.SemaphoreType.DMA((2,)),
             ],
             compiler_params=pltpu.CompilerParams(
                 collective_id=0, has_side_effects=True, vmem_limit_bytes=48 * 1024 * 1024

time: 56.8 us -> 54.4 us (0.958)
  Pallas kernels: 54.1 us -> 51.8 us
    pallas_call x1, Pallas kernels: 54.1 us -> 51.8 us  [step(): pl.pallas_call(functools.partial(kernel, count_s, count_p), out_shape=[pl...]
where the time goes in v3:
time: 54.4 us; the launch traced here: 53.8 us
  Pallas kernels  51.8 us (95%)
  local copies, waits for them, and re-layouts  1.36 us (2%)
  between operations  0.64 us (1%)
    pallas_call x1, Pallas kernels, step(): pl.pallas_call(functools.partial(kernel, count_s, count_p), out_shape=[pl...  51.8 us
    unnamed x2, local copies, waits for them, and re-layouts  1.36 us

profile of v3, /device:TPU:1, one launch (start us, length us, event | category | flops | bytes accessed | tf_op | source)
XLA Modules:
  0.0 53.8 jit_solution(14810262256354337988)
XLA Ops:
  0.6 51.8 %shard_map.59 = (f32[16,24,128]{2,1,0:T(8,128)S(1)}, f32[16,24,128]{2,1,0:T(8,128)S(1)}) custom-call(f32[16,24,128]{2,1,0:T(8,128)} %source_hbm.1, bf16[6,16,24,128]{3,2,1,0:T(8,128)(2,1)} %geometry_hbm.1, f32[16,128]{1,0:T(8,128)} %constant.4.clone.constant_hbm, bf16[4,128,128]{2,1,0:T(8,128)(2,1)} %constant.5.clone.matrix_hbm), custom_call_target="tpu_custom_call" | custom-call | tf_op jit(solution)/shard_map/pallas_call | solution.py:650
  52.4 0.7 %copy.8 = f32[16,24,128]{2,1,0:T(8,128)} copy(f32[16,24,128]{2,1,0:T(8,128)S(1)} %get-tuple-element.2) | data formatting | bytes 393216
  53.1 0.7 %copy.9 = f32[16,24,128]{2,1,0:T(8,128)} copy(f32[16,24,128]{2,1,0:T(8,128)S(1)} %get-tuple-element.3) | data formatting | bytes 393216

commit v4 on v3

--- a/solution.py
+++ b/solution.py
@@ -640,6 +640,17 @@
         whole(column.at[pl.ds(0, len(heads))], 0).wait_send()
 
 
+def store(a, b, a_out, b_out, sem):
+    copies = [
+        pltpu.make_async_copy(a, a_out, sem.at[0]),
+        pltpu.make_async_copy(b, b_out, sem.at[1]),
+    ]
+    for copy in copies:
+        copy.start()
+    for copy in copies:
+        copy.wait()
+
+
 def solution(mesh):
     count_s, count_p = mesh.shape["stream"], mesh.shape["span"]
 
@@ -647,7 +658,7 @@
         block = (EX * NODES, EY * NODES, LANES)
         in_hbm = pl.BlockSpec(memory_space=pltpu.HBM)
         f32 = jnp.float32
-        return pl.pallas_call(
+        pair = pl.pallas_call(
             functools.partial(kernel, count_s, count_p),
             out_shape=[pltpu.VMEM(block, f32)] * 2,
             in_specs=[in_hbm] * 4,
@@ -687,6 +698,13 @@
                 collective_id=0, has_side_effects=True, vmem_limit_bytes=48 * 1024 * 1024
             ),
         )(*(pltpu.with_memory_space_constraint(v, pltpu.HBM) for v in (source, geometry, jnp.asarray(constants()), jnp.asarray(matrices()))))
+        return pl.pallas_call(
+            store,
+            out_shape=[pltpu.HBM(block, f32)] * 2,
+            in_specs=[pl.BlockSpec(memory_space=pltpu.VMEM)] * 2,
+            out_specs=[in_hbm] * 2,
+            scratch_shapes=[pltpu.SemaphoreType.DMA((2,))],
+        )(*(pltpu.with_memory_space_constraint(v, pltpu.VMEM) for v in pair))
 
     return jax.shard_map(
         step,

time: 54.4 us -> 53.8 us (0.989)
  local copies, waits for them, and re-layouts: 1.36 us -> 0 us
  Pallas kernels: 51.8 us -> 52.5 us
    unnamed x2 -> x0, local copies, waits for them, and re-layouts: 1.36 us -> none
    pallas_call x0 -> x1, Pallas kernels: none -> 0.76 us  [step(): pl.pallas_call(store, out_shape=[pltpu.HBM(block, f32)] * 2, in_specs=[pl...]
where the time goes in v4:
time: 53.8 us; the launch traced here: 53.2 us
  Pallas kernels  52.5 us (98%)
  between operations  0.64 us (1%)
    pallas_call x1, Pallas kernels, step(): pl.pallas_call(functools.partial(kernel, count_s, count_p), out_shape=[pl...  51.8 us

profile of v4, /device:TPU:1, one launch (start us, length us, event | category | flops | bytes accessed | tf_op | source)
XLA Modules:
  0.0 53.2 jit_solution(15936282878067280038)
XLA Ops:
  0.6 51.8 %shard_map.59 = (f32[16,24,128]{2,1,0:T(8,128)S(1)}, f32[16,24,128]{2,1,0:T(8,128)S(1)}) custom-call(f32[16,24,128]{2,1,0:T(8,128)} %source_hbm.1, bf16[6,16,24,128]{3,2,1,0:T(8,128)(2,1)} %geometry_hbm.1, f32[16,128]{1,0:T(8,128)} %constant.4.clone.constant_hbm, bf16[4,128,128]{2,1,0:T(8,128)(2,1)} %constant.5.clone.matrix_hbm), custom_call_target="tpu_custom_call" | custom-call | tf_op jit(solution)/shard_map/pallas_call | solution.py:661
  52.4 0.8 %shard_map.60 = (f32[16,24,128]{2,1,0:T(8,128)}, f32[16,24,128]{2,1,0:T(8,128)}) custom-call(f32[16,24,128]{2,1,0:T(8,128)S(1)} %get-tuple-element.4.a, f32[16,24,128]{2,1,0:T(8,128)S(1)} %get-tuple-element.5.b), custom_call_target="tpu_custom_call" | custom-call | tf_op jit(solution)/shard_map/pallas_call | solution.py:701

commit v5 on v4

--- a/solution.py
+++ b/solution.py
@@ -353,7 +353,7 @@
                     grad2[x, rows, :] = f2
         return flux0, energy
 
-    def divergence(flux0, add=False):
+    def divergence(flux0, answer=None):
         flat = split(grad2[...].reshape(ROWS, LANES))
         along2 = along_z(flat, (matrix[0], matrix[1])).reshape(EX * NODES, EY * NODES, LANES)
         flat = split(grad1[...].reshape(ROWS, LANES))
@@ -368,7 +368,8 @@
                     total[x, e] = (
                         back[i] + grad1[x * EY + e] + along2[x, 8 * e : 8 * e + 8]
                     )
-        if add:
+        if answer is not None:
+            answer()
             for e in range(EY):
                 extra = response[8 * e : 8 * e + 8, :]
                 total[0, e] = total[0, e] + jnp.where(long_down, extra, 0.0)
@@ -428,13 +429,6 @@
 
     loads[0].wait()
     assemble(source[...], partial.at[0], packed.at[0])
-    pl.semaphore_wait(
-        barrier,
-        len(halo) + len(heads) + jnp.where(gathers, len(in_plane) - 1, 0),
-    )
-    flight = exchanges(0)
-    for copy in flight:
-        copy.start()
     loads[1].wait()
     loads[2].wait()
     loads[3].wait()
@@ -447,12 +441,27 @@
                     weight * float(WEIGHTS[x % NODES])
                 )
 
+
+    @pl.when(long_down)
+    def _():
+        describe_side(0, 0)
+
+    @pl.when(long_up)
+    def _():
+        describe_side(NODES, last)
+
+    pl.semaphore_wait(
+        barrier,
+        len(halo) + len(heads) + jnp.where(gathers, len(in_plane) - 1, 0),
+    )
+    flight = exchanges(0)
+    for copy in flight[::-1]:
+        copy.start()
+    pl.when(is_long)(side_copy().start)
     to_down, to_up = (0, 4, 5), (1, 6, 7)
     from_down, from_up = to_up, to_down
 
     def ahead(copies_from, copies_to, side_first, side_plane, **skip):
-        describe_side(side_first, side_plane)
-        side_copy().start()
         for i, copy in enumerate(flight):
             if i not in copies_from:
                 copy.wait_recv()
@@ -460,7 +469,7 @@
         face[...] = fields[0, side_plane]
         flux, _ = fluxes(0)
         assemble(divergence(flux), early, early_pack)
-        for i, copy in enumerate(exchanges(1, early, early_pack)):
+        for i, copy in list(enumerate(exchanges(1, early, early_pack)))[::-1]:
             if i in copies_to:
                 copy.start()
         for i, copy in enumerate(flight):
@@ -479,6 +488,12 @@
     def _():
         for copy in flight:
             copy.wait_recv()
+
+    def answer():
+        @pl.when(is_long)
+        def _():
+            side_copy().wait_recv()
+            respond()
 
     moments = []
     for k in range(ROUNDS - 1):
@@ -513,16 +528,10 @@
 
         for copy in flight:
             copy.wait_send()
-        if k == 0:
-
-            @pl.when(is_long)
-            def _():
-                side_copy().wait_recv()
-                respond()
-
-        assemble(divergence(flux0, k == 0), partial.at[k + 1], packed.at[k + 1])
+        values = divergence(flux0, answer if k == 0 else None)
+        assemble(values, partial.at[k + 1], packed.at[k + 1])
         flight = exchanges(k + 1)
-        for i, copy in enumerate(flight):
+        for i, copy in list(enumerate(flight))[::-1]:
             if k > 0 or i in (2, 3):
                 copy.start()
             else:

time: 53.8 us -> 53.8 us (level)
  no operation moved by 1% of the time
where the time goes in v5:
time: 53.8 us; the launch traced here: 53.1 us
  Pallas kernels  52.4 us (97%)
  between operations  0.64 us (1%)
    pallas_call x1, Pallas kernels, step(): pl.pallas_call(functools.partial(kernel, count_s, count_p), out_shape=[pl...  51.7 us

profile of v5, /device:TPU:1, one launch (start us, length us, event | category | flops | bytes accessed | tf_op | source)
XLA Modules:
  0.0 53.1 jit_solution(16547900644003019448)
XLA Ops:
  0.6 51.7 %shard_map.59 = (f32[16,24,128]{2,1,0:T(8,128)S(1)}, f32[16,24,128]{2,1,0:T(8,128)S(1)}) custom-call(f32[16,24,128]{2,1,0:T(8,128)} %source_hbm.1, bf16[6,16,24,128]{3,2,1,0:T(8,128)(2,1)} %geometry_hbm.1, f32[16,128]{1,0:T(8,128)} %constant.4.clone.constant_hbm, bf16[4,128,128]{2,1,0:T(8,128)(2,1)} %constant.5.clone.matrix_hbm), custom_call_target="tpu_custom_call" | custom-call | tf_op jit(solution)/shard_map/pallas_call | solution.py:670
  52.3 0.8 %shard_map.60 = (f32[16,24,128]{2,1,0:T(8,128)}, f32[16,24,128]{2,1,0:T(8,128)}) custom-call(f32[16,24,128]{2,1,0:T(8,128)S(1)} %get-tuple-element.4.a, f32[16,24,128]{2,1,0:T(8,128)S(1)} %get-tuple-element.5.b), custom_call_target="tpu_custom_call" | custom-call | tf_op jit(solution)/shard_map/pallas_call | solution.py:710
